TPU v7x, 32 devices: a whole 2x2x4 slice. The times are simulated.
32 devices in a mesh: dp: 2 (over y), section: 4 (over x, core), tensor: 4 (over z).
Axes of the slice: x: 2, y: 2, z: 4, core: 2. Of those that a mesh axis runs over, the one named last changes fastest.
Arguments:
- sent_cot: bfloat16 [2, 4, 2, 56, 8192], P('dp', 'section', None, 'tensor'), may hold values from -6 to 6
- saved_heads: bfloat16 [2, 4, 2, 56, 1024], P('dp', 'section', None, None, 'tensor'), may hold values from -0.29882812 to 0.29882812
- out_proj: bfloat16 [4, 8192, 1024], P('section', None, 'tensor'), may hold values from -0.0625 to 0.0625
Outputs:
- head_grads: bfloat16 [2, 4, 2, 56, 1024], P('dp', 'section', None, None, 'tensor')
- proj_grad: bfloat16 [4, 8192, 1024], P('section', 'dp', 'tensor')
All inputs are finite; a program needn't handle non-finite values.
Results may differ from a plain program's by a relative error of at most 0.013.
Values may be sent and summed in bfloat16 or wider, within the bound.
A program may use at most 64 MiB of HBM per device.

v0:
```python
import jax
import jax.numpy as jnp
from jax import lax
from jax.sharding import PartitionSpec as P


def from_behind(value, axis, steps):
    count = lax.axis_size(axis)
    pairs = [(source, (source + steps) % count) for source in range(count)]
    return lax.ppermute(value, axis, pairs)


def per_device(sent_cot, saved_heads, out_proj):
    local_cot = sent_cot[0, 0]
    head_rows = saved_heads[0, 0]
    weight = out_proj[0]
    from_above = from_behind(local_cot[0], "section", -1)
    from_below = from_behind(local_cot[1], "section", 1)
    incoming = jnp.stack([from_above, from_below])
    portion = lax.all_gather(incoming, "tensor", axis=1, tiled=True)
    grad_total = jnp.einsum("rkd,rkh->dh", portion, head_rows, preferred_element_type=jnp.float32)
    head_piece = jnp.einsum("rkd,dh->rkh", portion, weight, preferred_element_type=jnp.float32)
    head_total = head_piece
    grad_total, head_total = (grad_total, head_total)
    rounded = grad_total.astype(jnp.bfloat16).astype(jnp.float32)
    proj_share = lax.psum_scatter(
        rounded.astype(jnp.bfloat16), "dp", scatter_dimension=0, tiled=True
    )
    head_out = head_total.astype(jnp.bfloat16)
    return (head_out[None, None], proj_share[None])


def solution(mesh):
    return jax.shard_map(
        per_device,
        mesh=mesh,
        in_specs=(
            P("dp", "section", None, "tensor", None),
            P("dp", "section", None, None, "tensor"),
            P("section", None, "tensor"),
        ),
        out_specs=(P("dp", "section", None, None, "tensor"), P("section", "dp", "tensor")),
        check_vma=False,
    )
```

profile of v0, /device:TPU:0, one launch (start us, length us, event | category | flops | bytes accessed | tf_op | source)
XLA Modules:
  0.0 129.3 jit_solution(666977936013127331)
XLA Ops:
  7.2 0.0 copy-start
  7.2 0.0 all-gather.2.cloned.1.call-start
  7.2 2.1 %fusion.16 = (bf16[1,1,1,14,8192]{4,2,3,1,0:T(2,128)(2,1)S(1)}, bf16[1,1,1,14,8192]{4,2,3,1,0:T(2,128)(2,1)S(1)}) fusion(bf16[1,1,2,14,8192]{4,2,3,1,0:T(2,128)(2,1)} %param.3), kind=kLoop, calls=%fused_computation.12 | loop fusion | bytes 917504 | tf_op jit(solution)/shard_map/slice | solution.py:17
  9.3 0.3 copy.28
  9.6 0.5 collective-permute-start.1
  10.1 0.2 copy.29
  10.4 2.0 %collective-permute-start = (bf16[14,8192]{1,0:T(8,128)(2,1)S(1)}, bf16[14,8192]{1,0:T(8,128)(2,1)S(1)}, u32[]{:S(2)}, u32[]{:S(2)}) collective-permute-start(bf16[14,8192]{1,0:T(8,128)(2,1)S(1)} %bitcast.29), channel_id=1, source_target_pairs={{0,12},{4,0},{8,4},{12,8},{1,13},{5,1},{9,5},{13,9},{2,14},{6,2},{... | collective-permute-start | bytes 688136 | tf_op jit(solution)/shard_map/ppermute | solution.py:10
  12.4 3.7 %collective-permute-done.1 = bf16[14,8192]{1,0:T(8,128)(2,1)S(1)} collective-permute-done((bf16[14,8192]{1,0:T(8,128)(2,1)S(1)}, bf16[14,8192]{1,0:T(8,128)(2,1)S(1)}, u32[]{:S(2)}, u32[]{:S(2)}) %collective-permute-start.1) | collective-permute-done | bytes 229408 | tf_op jit(solution)/shard_map/ppermute | solution.py:10
  16.1 2.6 %collective-permute-done = bf16[14,8192]{1,0:T(8,128)(2,1)S(1)} collective-permute-done((bf16[14,8192]{1,0:T(8,128)(2,1)S(1)}, bf16[14,8192]{1,0:T(8,128)(2,1)S(1)}, u32[]{:S(2)}, u32[]{:S(2)}) %collective-permute-start) | collective-permute-done | bytes 229408 | tf_op jit(solution)/shard_map/ppermute | solution.py:10
  18.7 0.1 pad_maximum_fusion
  18.8 1.2 copy.13
  20.0 0.0 all-gather.2.cloned.1.call-update
  20.1 0.0 reduce-scatter.2.cloned.1.call-start
  20.1 43.2 %all-gather.2.cloned.1.call-done = bf16[2,56,8192]{2,0,1:T(2,128)(2,1)} async-done(((bf16[2,14,8192]{2,0,1:T(2,128)(2,1)}), bf16[2,56,8192]{2,0,1:T(2,128)(2,1)}) %all-gather.2.cloned.1.call-update) | async-done | bytes 1835024 | tf_op jit(solution)/shard_map/all_gather | solution.py:20
  63.3 0.0 copy-done
  63.3 5.8 %fusion = bf16[8192,256]{1,0:T(8,128)(2,1)} fusion(bf16[2,56,8192]{2,0,1:T(2,128)(2,1)} %all-gather.2.cloned.1.call-done, bf16[1,1,2,56,256]{4,3,2,1,0:T(8,128)(2,1)S(1)} %copy-done), kind=kOutput, calls=%fused_computation.1 | convolution fusion | flops 471859200 | bytes 6086656 | tf_op jit(solution)/shard_map/rkd,rkh->dh/dot_general | solution.py:21
  69.1 0.0 copy-start.1
  69.1 0.0 reduce-scatter.2.cloned.1.call-update
  69.1 1.5 %copy-done.1 = bf16[2,56,8192]{2,0,1:T(2,128)(2,1)S(1)} copy-done((bf16[2,56,8192]{2,0,1:T(2,128)(2,1)S(1)}, bf16[2,56,8192]{2,0,1:T(2,128)(2,1)}, u32[]{:S(2)}) %copy-start.1) | copy-done | bytes 1835032
  70.6 5.3 %fusion.10 = bf16[1,1,2,56,256]{4,3,2,1,0:T(8,128)(2,1)} fusion(bf16[1,8192,256]{2,1,0:T(8,128)(2,1)} %param.5, bf16[2,56,8192]{2,0,1:T(2,128)(2,1)S(1)} %copy-done.1), kind=kOutput, calls=%fused_computation.7 | convolution fusion | flops 469790720 | bytes 6086656 | tf_op jit(solution)/shard_map/rkd,dh->rkh/dot_general | solution.py:22
  75.8 46.6 %reduce-scatter.2.cloned.1.call-done = bf16[4096,256]{1,0:T(8,128)(2,1)} async-done(((bf16[8192,256]{1,0:T(8,128)(2,1)}), bf16[4096,256]{1,0:T(8,128)(2,1)}) %reduce-scatter.2.cloned.1.call-update) | async-done | bytes 2097168 | tf_op jit(solution)/shard_map/reduce_scatter | solution.py:26
Async XLA Ops:
  7.2 56.2 %copy-start = (bf16[1,1,2,56,256]{4,3,2,1,0:T(8,128)(2,1)S(1)}, bf16[1,1,2,56,256]{4,3,2,1,0:T(8,128)(2,1)}, u32[]{:S(2)}) copy-start(bf16[1,1,2,56,256]{4,3,2,1,0:T(8,128)(2,1)} %param.4) | copy-start | bytes 172036
  7.2 56.1 %all-gather.2.cloned.1.call-start = ((), (), s32[]{:S(2)}) async-start(), calls=%async_computation.1 | async-start | bytes 2293760 | tf_op jit(solution)/shard_map/all_gather | solution.py:20
  9.6 6.5 %collective-permute-start.1 = (bf16[14,8192]{1,0:T(8,128)(2,1)S(1)}, bf16[14,8192]{1,0:T(8,128)(2,1)S(1)}, u32[]{:S(2)}, u32[]{:S(2)}) collective-permute-start(bf16[14,8192]{1,0:T(8,128)(2,1)S(1)} %bitcast.27), channel_id=1, source_target_pairs={{0,4},{4,8},{8,12},{12,0},{1,5},{5,9},{9,13},{13,1},{2,6},{6,10},{... | collective-permute-start | bytes 688136 | tf_op jit(solution)/shard_map/ppermute | solution.py:10
  10.4 8.4 %collective-permute-start = (bf16[14,8192]{1,0:T(8,128)(2,1)S(1)}, bf16[14,8192]{1,0:T(8,128)(2,1)S(1)}, u32[]{:S(2)}, u32[]{:S(2)}) collective-permute-start(bf16[14,8192]{1,0:T(8,128)(2,1)S(1)} %bitcast.29), channel_id=1, source_target_pairs={{0,12},{4,0},{8,4},{12,8},{1,13},{5,1},{9,5},{13,9},{2,14},{6,2},{... | collective-permute-start | bytes 688136 | tf_op jit(solution)/shard_map/ppermute | solution.py:10
  20.1 102.4 %reduce-scatter.2.cloned.1.call-start = ((), (), s32[]{:S(2)}) async-start(), calls=%async_computation.2 | async-start | bytes 6291456 | tf_op jit(solution)/shard_map/reduce_scatter | solution.py:26
  69.1 1.5 %copy-start.1 = (bf16[2,56,8192]{2,0,1:T(2,128)(2,1)S(1)}, bf16[2,56,8192]{2,0,1:T(2,128)(2,1)}, u32[]{:S(2)}) copy-start(bf16[2,56,8192]{2,0,1:T(2,128)(2,1)} %all-gather.2.cloned.1.call-done) | copy-start | bytes 5505028
Sparse Core Ops, SparseCore 0:
  20.2 43.0 all-gather.1
  69.2 53.1 reduce-scatter.1
where the time goes:
time: 130 us; the launch traced here: 129 us
  waiting for transfers between devices  96.2 us (74%)
  between operations  14.1 us (11%)
  matrix products  11 us (8%)
  local copies, waits for them, and re-layouts  5.34 us (4%)
  starting transfers between devices  2.58 us (2%)
    reduce_scatter x1, waiting for transfers between devices, per_device(): lax.psum_scatter(rounded.astype(jnp.bfloat16), 'dp', scatter_dimension=0,...  46.6 us
    all_gather x1, waiting for transfers between devices, per_device(): portion = lax.all_gather(incoming, 'tensor', axis=1, tiled=True)  43.2 us
    ppermute x2, waiting for transfers between devices, from_behind(): return lax.ppermute(value, axis, pairs)  6.36 us
    dot_general x1, matrix products, per_device(): jnp.einsum('rkd,rkh->dh', portion, head_rows, preferred_element_type=jnp....  5.75 us
    dot_general x1, matrix products, per_device(): jnp.einsum('rkd,dh->rkh', portion, weight, preferred_element_type=jnp.flo...  5.27 us
  transfers between devices with their start and end apart: 4, of which 4 were waited for; matrix products, arithmetic and copies ran while one was open for 4% of the time, Pallas kernels for 0%

commit v1 on v0

--- a/solution.py
+++ b/solution.py
@@ -17,7 +17,14 @@
     from_above = from_behind(local_cot[0], "section", -1)
     from_below = from_behind(local_cot[1], "section", 1)
     incoming = jnp.stack([from_above, from_below])
-    portion = lax.all_gather(incoming, "tensor", axis=1, tiled=True)
+    ways, here = (lax.axis_size("tensor"), lax.axis_index("tensor"))
+    portion, reach = (incoming, 1)
+    while reach < ways:
+        theirs = lax.ppermute(portion, "tensor", [(d, d ^ reach) for d in range(ways)])
+        mine_first = jnp.concatenate([portion, theirs], axis=1)
+        theirs_first = jnp.concatenate([theirs, portion], axis=1)
+        portion = jnp.where(here & reach == 0, mine_first, theirs_first)
+        reach = 2 * reach
     grad_total = jnp.einsum("rkd,rkh->dh", portion, head_rows, preferred_element_type=jnp.float32)
     head_piece = jnp.einsum("rkd,dh->rkh", portion, weight, preferred_element_type=jnp.float32)
     head_total = head_piece

time: 130 us -> 144 us (1.11)
  waiting for transfers between devices: 96.2 us -> 111 us
  starting transfers between devices: 2.58 us -> 7 us
  matrix products: 11 us -> 7.2 us
    ppermute x0 -> x2, waiting for transfers between devices: none -> 53 us  [per_device(): lax.ppermute(portion, 'tensor', [(d, d ^ reach) for d in range(ways)])]
    all_gather x1 -> x0, waiting for transfers between devices: 43.2 us -> none  [per_device(): portion = lax.all_gather(incoming, 'tensor', axis=1, tiled=True)]
    reduce_scatter x1, waiting for transfers between devices: 46.6 us -> 51.9 us  [per_device(): lax.psum_scatter(rounded.astype(jnp.bfloat16), 'dp', scatter_dimension=0,...]
    ppermute x0 -> x2, starting transfers between devices: none -> 4.46 us  [per_device(): lax.ppermute(portion, 'tensor', [(d, d ^ reach) for d in range(ways)])]
    dot_general x1, matrix products: 5.75 us -> 3.27 us  [per_device(): jnp.einsum('rkd,rkh->dh', portion, head_rows, preferred_element_type=jnp....]
    unnamed x6 -> x4, local copies, waits for them, and re-layouts: 1.99 us -> 0.51 us
  transfers between devices with their start and end apart: 4 -> 5, of which waited for: 4 -> 5; matrix products, arithmetic and copies ran while one was open for 4% -> 3% of each run, Pallas kernels for 0% -> 0%
where the time goes in v1:
time: 144 us
  waiting for transfers between devices  111 us (77%)
  between operations  14.1 us (10%)
  matrix products  7.2 us (5%)
  starting transfers between devices  7 us (5%)
  local copies, waits for them, and re-layouts  4.08 us (3%)
    ppermute x2, waiting for transfers between devices, per_device(): lax.ppermute(portion, 'tensor', [(d, d ^ reach) for d in range(ways)])  53 us
    reduce_scatter x1, waiting for transfers between devices, per_device(): lax.psum_scatter(rounded.astype(jnp.bfloat16), 'dp', scatter_dimension=0,...  51.9 us
    ppermute x2, waiting for transfers between devices, from_behind(): return lax.ppermute(value, axis, pairs)  6.36 us
    ppermute x2, starting transfers between devices, per_device(): lax.ppermute(portion, 'tensor', [(d, d ^ reach) for d in range(ways)])  4.46 us
    dot_general x1, matrix products, per_device(): jnp.einsum('rkd,dh->rkh', portion, weight, preferred_element_type=jnp.flo...  3.93 us
    dot_general x1, matrix products, per_device(): jnp.einsum('rkd,rkh->dh', portion, head_rows, preferred_element_type=jnp....  3.27 us
  transfers between devices with their start and end apart: 5, of which 5 were waited for; matrix products, arithmetic and copies ran while one was open for 3% of the time, Pallas kernels for 0%

profile of v1, /device:TPU:0, one launch (start us, length us, event | category | flops | bytes accessed | tf_op | source)
XLA Modules:
  0.0 144.2 jit_solution(17994715579120791959)
XLA Ops:
  7.2 0.0 copy-start
  7.2 0.0 reduce-scatter.2.cloned.1.call-start
  7.2 2.1 %fusion.12 = (bf16[1,1,1,14,8192]{4,2,3,1,0:T(2,128)(2,1)S(1)}, bf16[1,1,1,14,8192]{4,2,3,1,0:T(2,128)(2,1)S(1)}) fusion(bf16[1,1,2,14,8192]{4,2,3,1,0:T(2,128)(2,1)} %param.3), kind=kLoop, calls=%fused_computation.14 | loop fusion | bytes 917504 | tf_op jit(solution)/shard_map/slice | solution.py:17
  9.3 0.3 copy.17
  9.6 0.5 collective-permute-start.1
  10.1 0.2 copy.18
  10.4 2.0 %collective-permute-start = (bf16[14,8192]{1,0:T(8,128)(2,1)S(1)}, bf16[14,8192]{1,0:T(8,128)(2,1)S(1)}, u32[]{:S(2)}, u32[]{:S(2)}) collective-permute-start(bf16[14,8192]{1,0:T(8,128)(2,1)S(1)} %bitcast.31), channel_id=1, source_target_pairs={{0,12},{4,0},{8,4},{12,8},{1,13},{5,1},{9,5},{13,9},{2,14},{6,2},{... | collective-permute-start | bytes 688136 | tf_op jit(solution)/shard_map/ppermute | solution.py:10
  12.4 3.7 %collective-permute-done.1 = bf16[14,8192]{1,0:T(8,128)(2,1)S(1)} collective-permute-done((bf16[14,8192]{1,0:T(8,128)(2,1)S(1)}, bf16[14,8192]{1,0:T(8,128)(2,1)S(1)}, u32[]{:S(2)}, u32[]{:S(2)}) %collective-permute-start.1) | collective-permute-done | bytes 229408 | tf_op jit(solution)/shard_map/ppermute | solution.py:10
  16.1 2.6 %collective-permute-done = bf16[14,8192]{1,0:T(8,128)(2,1)S(1)} collective-permute-done((bf16[14,8192]{1,0:T(8,128)(2,1)S(1)}, bf16[14,8192]{1,0:T(8,128)(2,1)S(1)}, u32[]{:S(2)}, u32[]{:S(2)}) %collective-permute-start) | collective-permute-done | bytes 229408 | tf_op jit(solution)/shard_map/ppermute | solution.py:10
  18.7 0.1 pad_maximum_fusion
  18.8 1.6 %collective-permute-start.2 = (bf16[2,14,8192]{2,1,0:T(8,128)(2,1)S(1)}, bf16[2,14,8192]{2,1,0:T(8,128)(2,1)S(1)}, u32[]{:S(2)}, u32[]{:S(2)}) collective-permute-start(bf16[2,14,8192]{2,1,0:T(8,128)(2,1)S(1)} %pad_maximum_fusion), channel_id=1, source_target_pairs={{0,1},{1,0},{2,3},{3,2},{4,5},{5,4},{6,7},{7,6},{8,9},{9,8},{10,11... | collective-permute-start | bytes 1376264 | tf_op jit(solution)/shard_map/ppermute | solution.py:23
  20.4 12.9 %collective-permute-done.2 = bf16[2,14,8192]{2,1,0:T(8,128)(2,1)S(1)} collective-permute-done((bf16[2,14,8192]{2,1,0:T(8,128)(2,1)S(1)}, bf16[2,14,8192]{2,1,0:T(8,128)(2,1)S(1)}, u32[]{:S(2)}, u32[]{:S(2)}) %collective-permute-start.2) | collective-permute-done | bytes 458784 | tf_op jit(solution)/shard_map/ppermute | solution.py:23
  33.3 0.5 maximum_select_fusion.1
  33.8 0.9 copy.10
  34.8 2.8 %collective-permute-start.3 = (bf16[2,28,8192]{2,0,1:T(2,128)(2,1)S(1)}, bf16[2,28,8192]{2,0,1:T(2,128)(2,1)S(1)}, u32[]{:S(2)}, u32[]{:S(2)}) collective-permute-start(bf16[2,28,8192]{2,0,1:T(2,128)(2,1)S(1)} %copy.10), channel_id=1, source_target_pairs={{0,2},{1,3},{2,0},{3,1},{4,6},{5,7},{6,4},{7,5},{8,10},{9,11},{10,... | collective-permute-start | bytes 2752520 | tf_op jit(solution)/shard_map/ppermute | solution.py:23
  37.6 40.1 %collective-permute-done.3 = bf16[2,28,8192]{2,0,1:T(2,128)(2,1)S(1)} collective-permute-done((bf16[2,28,8192]{2,0,1:T(2,128)(2,1)S(1)}, bf16[2,28,8192]{2,0,1:T(2,128)(2,1)S(1)}, u32[]{:S(2)}, u32[]{:S(2)}) %collective-permute-start.3) | collective-permute-done | bytes 917536 | tf_op jit(solution)/shard_map/ppermute | solution.py:23
  77.7 0.5 copy.11
  78.2 0.0 copy-done
  78.2 3.3 %fusion = bf16[8192,256]{1,0:T(8,128)(2,1)} fusion(bf16[2,28,8192]{2,1,0:T(8,128)(2,1)S(1)} %copy.11, bf16[2,28,8192]{2,1,0:T(8,128)(2,1)S(1)} %maximum_select_fusion.1, pred[]{:T(512)S(6)} %eq.6, bf16[1,1,2,56,256]{4,3,2,1,0:T(8,128)(2,1)S(1)} %copy-done), kind=kOutput, calls=%fused_computation.1 | convolution fusion | flops 480116736 | bytes 6086657 | tf_op jit(solution)/shard_map/rkd,rkh->dh/dot_general | solution.py:28
  81.5 0.0 reduce-scatter.2.cloned.1.call-update
  81.5 3.9 %fusion.6 = bf16[1,1,2,56,256]{4,3,2,1,0:T(8,128)(2,1)} fusion(bf16[1,8192,256]{2,1,0:T(8,128)(2,1)} %param.5, bf16[2,28,8192]{2,1,0:T(8,128)(2,1)S(1)} %copy.11, bf16[2,28,8192]{2,1,0:T(8,128)(2,1)S(1)} %maximum_select_fusion.1, pred[]{:T(512)S(6)} %eq.6), kind=kOutput, calls=%fused_computation.6 | convolution fusion | flops 478048256 | bytes 6086657 | tf_op jit(solution)/shard_map/rkd,dh->rkh/dot_general | solution.py:29
  85.5 51.9 %reduce-scatter.2.cloned.1.call-done = bf16[4096,256]{1,0:T(8,128)(2,1)} async-done(((bf16[8192,256]{1,0:T(8,128)(2,1)}), bf16[4096,256]{1,0:T(8,128)(2,1)}) %reduce-scatter.2.cloned.1.call-update) | async-done | bytes 2097168 | tf_op jit(solution)/shard_map/reduce_scatter | solution.py:33
Async XLA Ops:
  7.2 71.1 %copy-start = (bf16[1,1,2,56,256]{4,3,2,1,0:T(8,128)(2,1)S(1)}, bf16[1,1,2,56,256]{4,3,2,1,0:T(8,128)(2,1)}, u32[]{:S(2)}) copy-start(bf16[1,1,2,56,256]{4,3,2,1,0:T(8,128)(2,1)} %param.4) | copy-start | bytes 172036
  7.2 130.2 %reduce-scatter.2.cloned.1.call-start = ((), (), s32[]{:S(2)}) async-start(), calls=%async_computation.1 | async-start | bytes 6291456 | tf_op jit(solution)/shard_map/reduce_scatter | solution.py:33
  9.6 6.5 %collective-permute-start.1 = (bf16[14,8192]{1,0:T(8,128)(2,1)S(1)}, bf16[14,8192]{1,0:T(8,128)(2,1)S(1)}, u32[]{:S(2)}, u32[]{:S(2)}) collective-permute-start(bf16[14,8192]{1,0:T(8,128)(2,1)S(1)} %bitcast.30), channel_id=1, source_target_pairs={{0,4},{4,8},{8,12},{12,0},{1,5},{5,9},{9,13},{13,1},{2,6},{6,10},{... | collective-permute-start | bytes 688136 | tf_op jit(solution)/shard_map/ppermute | solution.py:10
  10.4 8.4 %collective-permute-start = (bf16[14,8192]{1,0:T(8,128)(2,1)S(1)}, bf16[14,8192]{1,0:T(8,128)(2,1)S(1)}, u32[]{:S(2)}, u32[]{:S(2)}) collective-permute-start(bf16[14,8192]{1,0:T(8,128)(2,1)S(1)} %bitcast.31), channel_id=1, source_target_pairs={{0,12},{4,0},{8,4},{12,8},{1,13},{5,1},{9,5},{13,9},{2,14},{6,2},{... | collective-permute-start | bytes 688136 | tf_op jit(solution)/shard_map/ppermute | solution.py:10
  18.8 14.5 %collective-permute-start.2 = (bf16[2,14,8192]{2,1,0:T(8,128)(2,1)S(1)}, bf16[2,14,8192]{2,1,0:T(8,128)(2,1)S(1)}, u32[]{:S(2)}, u32[]{:S(2)}) collective-permute-start(bf16[2,14,8192]{2,1,0:T(8,128)(2,1)S(1)} %pad_maximum_fusion), channel_id=1, source_target_pairs={{0,1},{1,0},{2,3},{3,2},{4,5},{5,4},{6,7},{7,6},{8,9},{9,8},{10,11... | collective-permute-start | bytes 1376264 | tf_op jit(solution)/shard_map/ppermute | solution.py:23
  34.8 43.0 %collective-permute-start.3 = (bf16[2,28,8192]{2,0,1:T(2,128)(2,1)S(1)}, bf16[2,28,8192]{2,0,1:T(2,128)(2,1)S(1)}, u32[]{:S(2)}, u32[]{:S(2)}) collective-permute-start(bf16[2,28,8192]{2,0,1:T(2,128)(2,1)S(1)} %copy.10), channel_id=1, source_target_pairs={{0,2},{1,3},{2,0},{3,1},{4,6},{5,7},{6,4},{7,5},{8,10},{9,11},{10,... | collective-permute-start | bytes 2752520 | tf_op jit(solution)/shard_map/ppermute | solution.py:23
Sparse Core Ops, SparseCore 0:
  81.7 55.6 reduce-scatter.1
